TPU v7x, 32 devices: a whole 2x2x4 slice. The times are simulated.
32 devices in a mesh: loader: 4 (over x, core), centers: 8 (over z, y).
Axes of the slice: x: 2, y: 2, z: 4, core: 2. Of those that a mesh axis runs over, the one named last changes fastest.
Arguments:
- pool: bfloat16 [32768, 256], P('loader'), may hold values from -6 to 6
- batch_index: int32 [2048], replicated, may hold values from 0 to 32767
- targets: float32 [16, 2048], replicated, may hold values from -6 to 6
- centers: bfloat16 [262144, 256], P(('loader', 'centers')), may hold values from -6 to 6
- weights: float32 [16, 262144], P(None, ('loader', 'centers')), may hold values from -1.8 to 1.8
- nys_index: int32 [2048], P(('loader', 'centers')), may hold values from 0 to 8191, as said below
- eigvecs: float32 [2048, 128], P(('loader', 'centers')), may hold values from -0.125 to 0.125
- damping: float32 [128], replicated, may hold values from 1 to 30
Outputs:
- new_weights: float32 [16, 262144], P(None, ('loader', 'centers'))
- predictions: float32 [16, 2048], replicated
Inputs may be any that keep to these rules, and one draw needn't show every extreme that they name: `nys_index`: each device's block of 64 entries names distinct local rows of that device's own 8192 centers; entry k lies in [k * 128, (k + 1) * 128); the first is 0 and the last 8191.
All inputs are finite; a program needn't handle non-finite values.
Results may differ from a plain program's by a relative error of at most 0.0049.
Values may be sent and summed in bfloat16 or wider, within the bound.
A program may use at most 256 MiB of HBM per device.

v0:
```python
import math

import jax
import jax.numpy as jnp
from jax import lax
from jax.sharding import PartitionSpec as P

D = 256


def pick_rows(pool, wanted):
    held = pool.shape[0]
    local = wanted - lax.axis_index("loader") * held
    owned = (local >= 0) & (local < held)
    rows = pool[jnp.clip(local, 0, held - 1)]
    return jnp.where(owned[:, None], rows, jnp.zeros_like(rows))


def body(pool, batch_index, targets, centers, weights, nys_index, eigvecs, damping):
    total_rows = batch_index.shape[0]
    share = total_rows // lax.axis_size("centers")
    mine = lax.dynamic_slice_in_dim(batch_index, lax.axis_index("centers") * share, share)
    summed = lax.psum(pick_rows(pool, mine), "loader").astype(jnp.float32).astype(jnp.bfloat16)
    batch = lax.all_gather(summed, "centers", axis=0, tiled=True)
    cen_sq = jnp.sum(centers.astype(jnp.float32) * centers.astype(jnp.float32), axis=1)
    width = min(512, total_rows)

    def tile(rows):
        row_sq = jnp.sum(rows.astype(jnp.float32) * rows.astype(jnp.float32), axis=1)
        cross = jnp.dot(rows, centers.T, preferred_element_type=jnp.float32)
        dist_sq = row_sq[:, None] + cen_sq[None, :] - 2.0 * cross
        return jnp.exp(-4.0 * jnp.sqrt(dist_sq) / math.sqrt(D)).astype(jnp.bfloat16)

    kern = lax.map(tile, batch.reshape(total_rows // width, width, batch.shape[1]))
    kern = kern.reshape(total_rows, centers.shape[0])
    w_half = weights.astype(jnp.bfloat16)
    partial_value = lax.dot_general(
        w_half, kern, (((1,), (1,)), ((), ())), preferred_element_type=jnp.float32
    )
    predictions = lax.psum(partial_value, ("loader", "centers"))
    resid = (predictions - targets).astype(jnp.bfloat16)
    grad = jnp.dot(resid, kern, preferred_element_type=jnp.float32)
    grad_nys = grad[:, nys_index]
    local_coeff = jnp.dot(
        grad_nys, eigvecs, precision=lax.Precision.HIGHEST, preferred_element_type=jnp.float32
    )
    coeff = lax.psum(local_coeff, ("loader", "centers"))
    delta = jnp.dot(
        coeff * damping[None, :],
        eigvecs.T,
        precision=lax.Precision.HIGHEST,
        preferred_element_type=jnp.float32,
    )
    fresh = weights - 2.0 * grad
    fresh = fresh.at[:, nys_index].add(2.0 * delta)
    return (fresh, predictions)


def solution(mesh):
    return jax.shard_map(
        body,
        mesh=mesh,
        in_specs=(
            P("loader", None),
            P(),
            P(),
            P(("loader", "centers"), None),
            P(None, ("loader", "centers")),
            P(("loader", "centers")),
            P(("loader", "centers"), None),
            P(),
        ),
        out_specs=(P(None, ("loader", "centers")), P()),
        check_vma=False,
    )
```

profile of v0, /device:TPU:0, one launch (start us, length us, event | category | flops | bytes accessed | tf_op | source)
XLA Modules:
  0.0 363.7 jit_solution(7236716942438408661)
XLA Ops:
  7.2 0.0 copy-start
  7.2 0.0 all-reduce.3.cloned.1.call-start
  7.2 0.8 compare_select_fusion
  8.0 0.8 compare_and_fusion
  8.8 3.7 %gather_fusion = bf16[256,256]{1,0:T(8,128)(2,1)S(1)} fusion(bf16[8192,256]{1,0:T(8,128)(2,1)} %param.10, s32[1024]{0:T(1024)S(1)} %pad_clamp_fusion.1), kind=kCustom, calls=%fused_computation | custom fusion | bytes 263168 | tf_op jit(solution)/shard_map/gather | solution.py:15
  12.5 0.8 broadcast_select_fusion
  13.2 0.0 all-reduce.3.cloned.1.call-update
  13.3 0.0 all-gather.2.cloned.1.call-start
  13.3 34.2 %all-reduce.3.cloned.1.call-done = bf16[256,256]{1,0:T(8,128)(2,1)} async-done(((bf16[256,256]{1,0:T(8,128)(2,1)}), bf16[256,256]{1,0:T(8,128)(2,1)}) %all-reduce.3.cloned.1.call-update) | async-done | bytes 131088 | tf_op jit(solution)/shard_map/psum | solution.py:23
  47.5 0.0 all-gather.2.cloned.1.call-update
  47.5 0.0 all-reduce.5.cloned.1.call-start
  47.6 0.7 compare_select_fusion.1
  48.3 3.3 multiply_reduce_fusion.1
  51.6 38.4 %all-gather.2.cloned.1.call-done = bf16[2048,256]{1,0:T(8,128)(2,1)} async-done(((bf16[256,256]{1,0:T(8,128)(2,1)}), bf16[2048,256]{1,0:T(8,128)(2,1)}) %all-gather.2.cloned.1.call-update) | async-done | bytes 1048592 | tf_op jit(solution)/shard_map/all_gather | solution.py:24
  90.0 0.0 copy-start.1
  90.0 58.4 %while.12 = (s32[]{:T(128)}, bf16[4,512,8192]{2,1,0:T(8,128)(2,1)}, bf16[4,512,256]{2,1,0:T(8,128)(2,1)}, f32[8192]{0:T(1024)S(1)}, bf16[8192,256]{1,0:T(8,128)(2,1)}, /*index=5*/s32[]{:T(128)}) while((s32[]{:T(128)}, bf16[4,512,8192]{2,1,0:T(8,128)(2,1)}, bf16[4,512,256]{2,1,0:T(8,128)(2,1)}, f32[8192]{0:T(1024)S(1)}, ...), condition=%wide.region_4.5_spmd, body=%wide.region_2.4_spmd.sunk | while | flops 2168847872 | bytes 13145161 | solution.py:34
  90.0 1.2 multiply_reduce_fusion.3
  91.2 13.5 %fusion.22 = bf16[4,512,8192]{2,1,0:T(8,128)(2,1)} fusion(bf16[4,512,8192]{2,1,0:T(8,128)(2,1)} %get-tuple-element.120, s32[]{:T(128)} %get-tuple-element.119, bf16[8192,256]{1,0:T(8,128)(2,1)} %get-tuple-element.129, f32[8192]{0:T(1024)S(1)} %get-tuple-element.128, f32[512]{0:T(512)S(1)} %multiply_reduce_fusion.3, ...), kind=kOutput, calls=%fused_computation.5.clone.1 | convolution fusion | flops 2168455168 | bytes 12880896 | tf_op jit(solution)/shard_map/while/body/eval_jaxpr/dot_general | solution.py:30
  104.7 1.1 multiply_reduce_fusion.3
  105.8 13.5 %fusion.22 = bf16[4,512,8192]{2,1,0:T(8,128)(2,1)} fusion(bf16[4,512,8192]{2,1,0:T(8,128)(2,1)} %get-tuple-element.120, s32[]{:T(128)} %get-tuple-element.119, bf16[8192,256]{1,0:T(8,128)(2,1)} %get-tuple-element.129, f32[8192]{0:T(1024)S(1)} %get-tuple-element.128, f32[512]{0:T(512)S(1)} %multiply_reduce_fusion.3, ...), kind=kOutput, calls=%fused_computation.5.clone.1 | convolution fusion | flops 2168455168 | bytes 12880896 | tf_op jit(solution)/shard_map/while/body/eval_jaxpr/dot_general | solution.py:30
  119.3 1.1 multiply_reduce_fusion.3
  120.4 13.5 %fusion.22 = bf16[4,512,8192]{2,1,0:T(8,128)(2,1)} fusion(bf16[4,512,8192]{2,1,0:T(8,128)(2,1)} %get-tuple-element.120, s32[]{:T(128)} %get-tuple-element.119, bf16[8192,256]{1,0:T(8,128)(2,1)} %get-tuple-element.129, f32[8192]{0:T(1024)S(1)} %get-tuple-element.128, f32[512]{0:T(512)S(1)} %multiply_reduce_fusion.3, ...), kind=kOutput, calls=%fused_computation.5.clone.1 | convolution fusion | flops 2168455168 | bytes 12880896 | tf_op jit(solution)/shard_map/while/body/eval_jaxpr/dot_general | solution.py:30
  133.9 1.1 multiply_reduce_fusion.3
  135.0 13.5 %fusion.22 = bf16[4,512,8192]{2,1,0:T(8,128)(2,1)} fusion(bf16[4,512,8192]{2,1,0:T(8,128)(2,1)} %get-tuple-element.120, s32[]{:T(128)} %get-tuple-element.119, bf16[8192,256]{1,0:T(8,128)(2,1)} %get-tuple-element.129, f32[8192]{0:T(1024)S(1)} %get-tuple-element.128, f32[512]{0:T(512)S(1)} %multiply_reduce_fusion.3, ...), kind=kOutput, calls=%fused_computation.5.clone.1 | convolution fusion | flops 2168455168 | bytes 12880896 | tf_op jit(solution)/shard_map/while/body/eval_jaxpr/dot_general | solution.py:30
  148.5 0.0 copy-done.1
  148.5 0.0 copy-start.3
  148.5 15.7 %convolution_bitcast_fusion = f32[16,2048]{1,0:T(8,128)} fusion(bf16[2048,8192]{1,0:T(8,128)(2,1)} %bitcast.28, f32[16,8192]{1,0:T(8,128)S(1)} %copy-done.1), kind=kOutput, calls=%fused_computation.11 | convolution fusion | flops 537001984 | bytes 34209792 | tf_op jit(solution)/shard_map/dot_general | solution.py:37
  164.1 0.0 all-reduce.5.cloned.1.call-update
  164.2 0.0 copy-start.4
  164.2 121.3 %all-reduce.5.cloned.1.call-done = f32[16,2048]{1,0:T(8,128)} async-done(((f32[16,2048]{1,0:T(8,128)}), f32[16,2048]{1,0:T(8,128)}) %all-reduce.5.cloned.1.call-update) | async-done | bytes 131088 | tf_op jit(solution)/shard_map/psum | solution.py:40
  285.5 0.0 copy-done.3
  285.5 0.0 copy-start.2
  285.5 14.8 %multiply_subtract_fusion = (f32[16,8192]{1,0:T(8,128)S(1)}, f32[16,8192]{1,0:T(8,128)S(1)}) fusion(f32[16,8192]{1,0:T(8,128)S(1)} %copy-done.1, bf16[2048,8192]{1,0:T(8,128)(2,1)} %bitcast.29, f32[16,2048]{1,0:T(8,128)} %all-reduce.5.cloned.1.call-done, f32[16,2048]{1,0:T(8,128)S(1)} %copy-done.3), kind=kOutput, calls=%fused_computation.14 | convolution fusion | flops 537198592 | bytes 35389440 | tf_op jit(solution)/shard_map/dot_general | solution.py:42
  300.3 2.6 copy.10
  302.9 2.8 gather_fusion.1
  305.7 0.0 copy-done
  305.7 0.2 fusion.10
  305.9 39.2 %psum.23 = f32[16,128]{1,0:T(8,128)S(1)} all-reduce(f32[16,128]{1,0:T(8,128)S(1)} %fusion.10), channel_id=1, replica_groups=mesh['loader'=4,'centers'=8] {'loader','centers'}, use_global_device_ids=true, to_apply=%region_6.7 | all-reduce | flops 2048 | bytes 16384 | tf_op jit(solution)/shard_map/psum | solution.py:47
  345.2 0.0 copy-done.4
  345.2 0.1 fusion.5
  345.3 0.1 copy.12
  345.4 2.6 copy.11
  348.0 4.9 %scatter_fusion = f32[16,8192]{0,1:T(8,128)} fusion(f32[16,8192]{0,1:T(8,128)} %copy.11, s32[64]{0:T(128)S(1)} %compare_select_fusion.1, f32[64,16]{1,0:T(8,128)S(1)} %copy.12), kind=kCustom, calls=%fused_computation.2 | custom fusion | flops 1024 | bytes 12544 | tf_op jit(solution)/shard_map/scatter-add | solution.py:55
  353.0 3.5 copy.13
  356.5 0.0 copy-done.2
  356.5 0.7 copy.26
  (3 shorter events, 0.0 us)
Async XLA Ops:
  7.2 298.6 %copy-start = (f32[64,128]{1,0:T(8,128)S(1)}, f32[64,128]{1,0:T(8,128)}, u32[]{:S(2)}) copy-start(f32[64,128]{1,0:T(8,128)} %param.16) | copy-start | bytes 98308
  7.2 40.3 %all-reduce.3.cloned.1.call-start = ((), (), s32[]{:S(2)}) async-start(), calls=%async_computation | async-start | bytes 262144 | tf_op jit(solution)/shard_map/psum | solution.py:23
  13.3 76.8 %all-gather.2.cloned.1.call-start = ((), (), s32[]{:S(2)}) async-start(), calls=%async_computation.1 | async-start | bytes 1179648 | tf_op jit(solution)/shard_map/all_gather | solution.py:24
  47.5 238.0 %all-reduce.5.cloned.1.call-start = ((), (), s32[]{:S(2)}) async-start(), calls=%async_computation.2 | async-start | bytes 262144 | tf_op jit(solution)/shard_map/psum | solution.py:40
  90.0 58.4 %copy-start.1 = (f32[16,8192]{1,0:T(8,128)S(1)}, f32[16,8192]{1,0:T(8,128)}, u32[]{:S(2)}) copy-start(f32[16,8192]{1,0:T(8,128)} %param.14) | copy-start | bytes 1572868
  148.5 137.0 %copy-start.3 = (f32[16,2048]{1,0:T(8,128)S(1)}, f32[16,2048]{1,0:T(8,128)}, u32[]{:S(2)}) copy-start(f32[16,2048]{1,0:T(8,128)} %param.12) | copy-start | bytes 393220
  164.2 181.0 %copy-start.4 = (f32[128]{0:T(128)S(1)}, f32[128]{0:T(128)}, u32[]{:S(2)}) copy-start(f32[128]{0:T(128)} %param.17) | copy-start | bytes 1540
  285.5 71.0 %copy-start.2 = (f32[16,2048]{1,0:T(8,128)S(1)}, f32[16,2048]{1,0:T(8,128)}, u32[]{:S(2)}) copy-start(f32[16,2048]{1,0:T(8,128)} %all-reduce.5.cloned.1.call-done) | copy-start | bytes 393220
Sparse Core Ops, SparseCore 0:
  13.4 34.0 all-reduce.2
  49.9 40.1 all-gather.1
  164.3 121.1 all-reduce.4
where the time goes:
time: 364 us
  waiting for transfers between devices  194 us (53%)
  matrix products  84.8 us (23%)
  blocking collectives  39.2 us (11%)
  local copies, waits for them, and re-layouts  16 us (4%)
  other arithmetic  15.7 us (4%)
  between operations  13.8 us (4%)
    psum x1, waiting for transfers between devices, body(): predictions = lax.psum(partial_value, ('loader', 'centers'))  121 us
    dot_general x4, matrix products, tile(): cross = jnp.dot(rows, centers.T, preferred_element_type=jnp.float32)  53.9 us
    psum x1, blocking collectives, body(): coeff = lax.psum(local_coeff, ('loader', 'centers'))  39.2 us
    all_gather x1, waiting for transfers between devices, body(): batch = lax.all_gather(summed, 'centers', axis=0, tiled=True)  38.4 us
    psum x1, waiting for transfers between devices, body(): lax.psum(pick_rows(pool, mine), 'loader').astype(jnp.float32)  34.2 us
    dot_general x1, matrix products, body(): lax.dot_general(w_half, kern, (((1,), (1,)), ((), ())), preferred_element...  15.7 us
    dot_general x1, matrix products, body(): grad = jnp.dot(resid, kern, preferred_element_type=jnp.float32)  14.8 us
  transfers between devices with their start and end apart: 3, of which 3 were waited for; matrix products, arithmetic and copies ran while one was open for 1% of the time, Pallas kernels for 0%

commit v1 on v0

v1 whole, which is shorter than its diff:
```python
import functools
import math

import jax
import jax.numpy as jnp
from jax import lax
from jax.experimental import pallas as pl
from jax.experimental.pallas import tpu as pltpu
from jax.sharding import PartitionSpec as P

PIECE = 16
SUB = 512
CT = 512
GT = 1024
PT = 512
F32, BF16 = jnp.float32, jnp.bfloat16
NT = (((1,), (1,)), ((), ()))
NN = (((1,), (0,)), ((), ()))


def dot(a, b, dims=NN):
    return lax.dot_general(a, b, dims, preferred_element_type=F32)


def kernel(
    nl, nc, nch,
    lidx_ref, nys_ref, targets_ref, eig_ref, damp_ref, pool_hbm, cen_hbm, w_hbm,
    out_ref, pred_ref,
    pool, cen, w, w_half, kern, cen_b, rows2, row_sq, batch, picked, pick_in, own,
    part, rs_in, cg_in, quarter, resid, grad, co_in, co_in2, co_own,
    sem_in, s_pick, r_pick, s_bc, r_bc, s_x, r_x, s_rs, r_rs, s_cg, r_cg, s_lg, r_lg,
    s_c1, r_c1, s_c2, r_c2,
):
    L = lax.axis_index("loader")
    c = lax.axis_index("centers")
    core_peer = L + 1 - 2 * lax.rem(L, 2)
    x_peer = L + 2 - 4 * lax.div(L, 2)
    lpeer = [lax.rem(L + d, nl) for d in range(1, nl)]
    cpeer = [lax.rem(c + d, nc) for d in range(1, nc)]
    n_cen = cen.shape[0]
    chunk = nl * nc * PIECE
    qw = nc * PIECE
    n_sub = chunk // SUB
    started = []

    def send(src, dst, ss, rs, loader, centers):
        copy = pltpu.make_async_remote_copy(
            src_ref=src, dst_ref=dst, send_sem=ss, recv_sem=rs,
            device_id=(loader, centers), device_id_type=pl.DeviceIdType.MESH,
        )
        copy.start()
        started.append(copy)
        return copy

    loads = [
        pltpu.make_async_copy(pool_hbm, pool, sem_in.at[0]),
        pltpu.make_async_copy(cen_hbm, cen, sem_in.at[1]),
        pltpu.make_async_copy(w_hbm, w, sem_in.at[2]),
    ]
    for load in loads:
        load.start()

    barrier = pltpu.get_barrier_semaphore()
    for p in lpeer:
        pl.semaphore_signal(barrier, inc=1, device_id=(p, c), device_id_type=pl.DeviceIdType.MESH)
    for p in cpeer:
        pl.semaphore_signal(barrier, inc=1, device_id=(L, p), device_id_type=pl.DeviceIdType.MESH)

    loads[0].wait()
    held = pool.shape[0]
    n_pick = lidx_ref.shape[0]
    lidx = lidx_ref[...] - L * held

    def pick(t, acc):
        spot = lax.broadcasted_iota(jnp.int32, (n_pick, PT), 1) + t * PT
        hot = jnp.where(spot == lidx, 1.0, 0.0).astype(BF16)
        return acc + dot(hot, pool[pl.ds(pl.multiple_of(t * PT, PT), PT), :])

    acc = lax.fori_loop(0, held // PT, pick, jnp.zeros((n_pick, pool.shape[1]), F32))
    picked[...] = acc.astype(BF16).reshape(picked.shape)
    pl.semaphore_wait(barrier, nl - 1 + nc - 1)
    copies = [
        send(picked.at[p], pick_in.at[L], s_pick.at[d], r_pick.at[d], p, c)
        for d, p in enumerate(lpeer)
    ]
    pick_in[L] = picked[L]

    loads[1].wait()
    ones = jnp.ones((cen.shape[1], 128), BF16)

    def norms(t, carry):
        at = pl.ds(pl.multiple_of(t * CT, CT), CT)
        sq = cen[at, :].astype(F32)
        sq = sq * sq
        hi = sq.astype(BF16)
        lo = (sq - hi.astype(F32)).astype(BF16)
        cen_b[at, :] = dot(hi, ones) + dot(lo, ones)
        return carry

    lax.fori_loop(0, n_cen // CT, norms, 0)
    loads[2].wait()
    w_half[...] = w[...].astype(BF16)

    for copy in copies:
        copy.wait_recv()
    total = pick_in[0].astype(F32)
    for p in range(1, nl):
        total = total + pick_in[p].astype(F32)
    own[...] = total.astype(BF16).reshape(own.shape)
    mine = pl.ds(pl.multiple_of(c * PIECE, PIECE), PIECE)
    bc = []
    for k in range(nch):
        bc.append([
            send(own.at[k], batch.at[k, L, mine], s_bc.at[k, d], r_bc.at[k, d], L, p)
            for d, p in enumerate(cpeer)
        ])
    for k in range(nch):
        batch[k, L, mine] = own[k]

    xs = {}

    def x_send(k):
        for copy in bc[k]:
            copy.wait_recv()
        block = batch.at[k, L]
        xs[k] = [
            send(block, block, s_x.at[k, 0], r_x.at[k, 0], x_peer, c),
            send(block, block, s_x.at[k, 1], r_x.at[k, 1], core_peer, c),
        ]

    def x_forward(k):
        xs[k][0].wait_recv()
        block = batch.at[k, x_peer]
        xs[k].append(send(block, block, s_x.at[k, 2], r_x.at[k, 2], core_peer, c))

    def x_done(k):
        xs[k][1].wait_recv()
        xs[k][2].wait_recv()

    rs, cg, lg = {}, {}, {}

    def ar_start(k):
        rs[k] = [
            send(part.at[k, p], rs_in.at[k, L], s_rs.at[k, d], r_rs.at[k, d], p, c)
            for d, p in enumerate(lpeer)
        ]
        rs_in[k, L] = part[k, L]

    def ar_mid(k):
        for copy in rs[k]:
            copy.wait_recv()
        cg_in[k, c] = sum((rs_in[k, p] for p in range(1, nl)), rs_in[k, 0])
        cg[k] = [
            send(cg_in.at[k, c], cg_in.at[k, c], s_cg.at[k, d], r_cg.at[k, d], L, p)
            for d, p in enumerate(cpeer)
        ]

    def ar_fin(k):
        for copy in cg[k]:
            copy.wait_recv()
        quarter[k, L] = sum((cg_in[k, p] for p in range(1, nc)), cg_in[k, 0])
        lg[k] = [
            send(quarter.at[k, L], quarter.at[k, L], s_lg.at[k, d], r_lg.at[k, d], p, c)
            for d, p in enumerate(lpeer)
        ]

    def residual(k):
        for copy in lg[k]:
            copy.wait_recv()
        for p in range(nl):
            lo = k * chunk + p * qw
            pred_ref[:, lo:lo + qw] = quarter[k, p]
            diff = quarter[k, p] - targets_ref[:, lo:lo + qw]
            resid[:, lo:lo + qw] = diff.astype(BF16)

    scale = -4.0 / math.sqrt(cen.shape[1]) * math.log2(math.e)

    def prepare(k):
        one = jnp.ones((8, cen.shape[1]), BF16)
        rows = batch[k].reshape(chunk, cen.shape[1])
        for s in range(n_sub):
            r = rows[s * SUB:(s + 1) * SUB].astype(F32)
            rows2[s] = (-2.0 * r).astype(BF16)
            sq = r * r
            hi = sq.astype(BF16)
            lo = (sq - hi.astype(F32)).astype(BF16)
            row_sq[s] = dot(one, hi, NT) + dot(one, lo, NT)

    def compute(k, half):
        tiles = n_cen // CT // 2
        for s in range(n_sub):
            def step(t, acc):
                at = pl.ds(pl.multiple_of((t + half * tiles) * CT, CT), CT)
                cross = dot(cen[at, :], rows2[s], NT)
                side = jnp.concatenate([cen_b[at, :]] * (SUB // 128), axis=1)
                z = jnp.maximum(cross + row_sq[s, 0:1, :] + side, 1e-30)
                val = jnp.exp2((z * lax.rsqrt(z)) * scale).astype(BF16)
                kern[k * n_sub + s, at, :] = val
                return acc + dot(w_half[:, at], val)

            acc = lax.fori_loop(0, tiles, step, jnp.zeros((16, SUB), F32))
            per = max(1, SUB // qw)
            width = min(qw, SUB)
            for q in range(per):
                lo = s * SUB + q * width
                dst = (k, lo // qw, slice(None), slice(lo % qw, lo % qw + width))
                piece = acc[:, q * width:(q + 1) * width]
                part[dst] = piece if half == 0 else part[dst] + piece

    def gradient(k):
        for s in range(n_sub):
            lo = k * chunk + s * SUB

            def step(t, carry):
                at = pl.ds(pl.multiple_of(t * GT, GT), GT)
                term = dot(resid[:, lo:lo + SUB], kern[k * n_sub + s, at, :], NT)
                if lo == 0:
                    grad[:, at] = term
                else:
                    grad[:, at] = grad[:, at] + term
                return carry

            lax.fori_loop(0, n_cen // GT, step, 0)

    x_send(0)
    x_forward(0)
    x_done(0)
    if nch > 1:
        x_send(1)
    for k in range(nch):
        prepare(k)
        compute(k, 0)
        if k + 1 < nch:
            x_forward(k + 1)
        if k >= 1:
            ar_mid(k - 1)
        compute(k, 1)
        if k + 1 < nch:
            x_done(k + 1)
        if k + 2 < nch:
            x_send(k + 2)
        ar_start(k)
        if k >= 1:
            ar_fin(k - 1)
    last = nch - 1
    for k in range(min(1, last)):
        residual(k)
        gradient(k)
    ar_mid(last)
    for k in range(1, min(2, last)):
        residual(k)
        gradient(k)
    ar_fin(last)
    for k in range(2, last):
        residual(k)
        gradient(k)
    residual(last)
    gradient(last)

    n_nys = eig_ref.shape[0]
    lane = lax.broadcasted_iota(jnp.int32, (16, 128), 1)

    def coeff_step(j, acc):
        at = pl.ds(pl.multiple_of(j * 128, 128), 128)
        hit = lane == nys_ref[j] - j * 128
        g = jnp.sum(jnp.where(hit, grad[:, at], 0.0), axis=1, keepdims=True)
        return acc + g * eig_ref[pl.ds(j, 1), :]

    co_own[0] = lax.fori_loop(0, n_nys, coeff_step, jnp.zeros((16, 128), F32), unroll=8)
    c1 = [
        send(co_own.at[0], co_in.at[L], s_c1.at[d], r_c1.at[d], p, c)
        for d, p in enumerate(lpeer)
    ]
    co_in[L] = co_own[0]
    for copy in c1:
        copy.wait_recv()
    co_own[1] = sum((co_in[p] for p in range(1, nl)), co_in[0])
    c2 = [
        send(co_own.at[1], co_in2.at[c], s_c2.at[d], r_c2.at[d], L, p)
        for d, p in enumerate(cpeer)
    ]
    co_in2[c] = co_own[1]
    for copy in c2:
        copy.wait_recv()
    coeff = sum((co_in2[p] for p in range(1, nc)), co_in2[0]) * damp_ref[...]

    def final_step(j, carry):
        at = pl.ds(pl.multiple_of(j * 128, 128), 128)
        hit = lane == nys_ref[j] - j * 128
        d = jnp.sum(coeff * eig_ref[pl.ds(j, 1), :], axis=1, keepdims=True)
        out_ref[:, at] = w[:, at] - 2.0 * grad[:, at] + jnp.where(hit, 2.0 * d, 0.0)
        return carry

    lax.fori_loop(0, n_nys, final_step, 0, unroll=8)
    for copy in started:
        copy.wait_send()


def body(pool, batch_index, targets, centers, weights, nys_index, eigvecs, damping):
    nl, nc = lax.axis_size("loader"), lax.axis_size("centers")
    rows = batch_index.shape[0]
    nch = rows // (nl * nc * PIECE)
    chunk = rows // nch
    width = centers.shape[1]
    n_cen = centers.shape[0]
    qw = nc * PIECE
    index = batch_index.reshape(nch, nl, nc, PIECE)
    index = lax.dynamic_slice_in_dim(index, lax.axis_index("centers"), 1, axis=2)
    lidx = jnp.transpose(index[:, :, 0, :], (1, 0, 2)).reshape(nl * nch * PIECE, 1)
    dma = lambda *s: [pltpu.SemaphoreType.DMA(s), pltpu.SemaphoreType.DMA(s)]
    vmem = pl.BlockSpec(memory_space=pltpu.VMEM)
    hbm = pl.BlockSpec(memory_space=pl.ANY)
    fresh, predictions = pl.pallas_call(
        functools.partial(kernel, nl, nc, nch),
        out_shape=(
            jax.ShapeDtypeStruct(weights.shape, F32),
            jax.ShapeDtypeStruct(targets.shape, F32),
        ),
        in_specs=[vmem, pl.BlockSpec(memory_space=pltpu.SMEM), vmem, vmem, vmem, hbm, hbm, hbm],
        out_specs=(vmem, vmem),
        scratch_shapes=[
            pltpu.VMEM(pool.shape, BF16),
            pltpu.VMEM(centers.shape, BF16),
            pltpu.VMEM(weights.shape, F32),
            pltpu.VMEM(weights.shape, BF16),
            pltpu.VMEM((rows // SUB, n_cen, SUB), BF16),
            pltpu.VMEM((n_cen, 128), F32),
            pltpu.VMEM((chunk // SUB, SUB, width), BF16),
            pltpu.VMEM((chunk // SUB, 8, SUB), F32),
            pltpu.VMEM((nch, nl, qw, width), BF16),
            pltpu.VMEM((nl, nch * PIECE, width), BF16),
            pltpu.VMEM((nl, nch * PIECE, width), BF16),
            pltpu.VMEM((nch, PIECE, width), BF16),
            pltpu.VMEM((nch, nl, 16, qw), F32),
            pltpu.VMEM((nch, nl, 16, qw), F32),
            pltpu.VMEM((nch, nc, 16, qw), F32),
            pltpu.VMEM((nch, nl, 16, qw), F32),
            pltpu.VMEM((16, rows), BF16),
            pltpu.VMEM(weights.shape, F32),
            pltpu.VMEM((nl, 16, 128), F32),
            pltpu.VMEM((nc, 16, 128), F32),
            pltpu.VMEM((2, 16, 128), F32),
            pltpu.SemaphoreType.DMA((3,)),
            *dma(nl - 1), *dma(nch, nc - 1), *dma(nch, 3), *dma(nch, nl - 1),
            *dma(nch, nc - 1), *dma(nch, nl - 1), *dma(nl - 1), *dma(nc - 1),
        ],
        compiler_params=pltpu.CompilerParams(
            collective_id=0, has_side_effects=True, vmem_limit_bytes=62 * 1024 * 1024
        ),
    )(lidx, nys_index, targets, eigvecs, damping.reshape(1, -1), pool, centers, weights)
    return (fresh, predictions)


def solution(mesh):
    return jax.shard_map(
        body,
        mesh=mesh,
        in_specs=(
            P("loader", None),
            P(),
            P(),
            P(("loader", "centers"), None),
            P(None, ("loader", "centers")),
            P(("loader", "centers")),
            P(("loader", "centers"), None),
            P(),
        ),
        out_specs=(P(None, ("loader", "centers")), P()),
        check_vma=False,
    )
```

time: 364 us -> 98.5 us (0.27)
  waiting for transfers between devices: 194 us -> 0 us
  Pallas kernels: 0 us -> 92.6 us
  matrix products: 84.8 us -> 0 us
  blocking collectives: 39.2 us -> 0 us
  other arithmetic: 15.7 us -> 0 us
  between operations: 13.8 us -> 0.66 us
  local copies, waits for them, and re-layouts: 16 us -> 4.99 us
    psum x2 -> x0, waiting for transfers between devices: 156 us -> none  [the longest x1 121 us: body(): predictions = lax.psum(partial_value, ('loader', 'centers'))]
    pallas_call x0 -> x1, Pallas kernels: none -> 92.6 us  [body(): pl.pallas_call(functools.partial(kernel, nl, nc, nch), out_shape=(jax.Sha...]
    dot_general x8 -> x0, matrix products: 84.8 us -> none  [the longest x4 53.9 us: tile(): cross = jnp.dot(rows, centers.T, preferred_element_type=jnp.float32)]
    psum x1 -> x0, blocking collectives: 39.2 us -> none  [body(): coeff = lax.psum(local_coeff, ('loader', 'centers'))]
    all_gather x1 -> x0, waiting for transfers between devices: 38.4 us -> none  [body(): batch = lax.all_gather(summed, 'centers', axis=0, tiled=True)]
    reduce_sum x5 -> x0, other arithmetic: 7.78 us -> none  [the longest x4 4.44 us: tile(): jnp.sum(rows.astype(jnp.float32) * rows.astype(jnp.float32), axis=1)]
    gather x2 -> x0, local copies, waits for them, and re-layouts: 6.48 us -> none  [the longest x1 3.7 us: pick_rows(): rows = pool[jnp.clip(local, 0, held - 1)]]
    scatter-add x1 -> x0, other arithmetic: 4.95 us -> none  [body(): fresh = fresh.at[:, nys_index].add(2.0 * delta)]
  transfers between devices with their start and end apart: 3 -> 0, of which waited for: 3 -> 0; matrix products, arithmetic and copies ran while one was open for 1% -> 0% of each run, Pallas kernels for 0% -> 0%
where the time goes in v1:
time: 98.5 us; the launch traced here: 98.3 us
  Pallas kernels  92.6 us (94%)
  local copies, waits for them, and re-layouts  4.99 us (5%)
    pallas_call x1, Pallas kernels, body(): pl.pallas_call(functools.partial(kernel, nl, nc, nch), out_shape=(jax.Sha...  92.6 us
    unnamed x2, local copies, waits for them, and re-layouts  3.44 us

profile of v1, /device:TPU:0, one launch (start us, length us, event | category | flops | bytes accessed | tf_op | source)
XLA Modules:
  0.0 98.3 jit_solution(6496371584592764504)
XLA Ops:
  0.6 0.8 reshape.13
  1.4 0.8 reshape.16.lidx_ref
  2.2 92.6 %shard_map.95 = (f32[16,8192]{1,0:T(8,128)}, f32[16,2048]{1,0:T(8,128)}) custom-call(s32[256,1]{1,0:T(8,128)} %reshape.16.lidx_ref, s32[64]{0:T(128)} %nys_ref.1, f32[16,2048]{1,0:T(8,128)} %targets_ref.1, f32[64,128]{1,0:T(8,128)} %eig_ref.1, f32[1,128]{1,0:T(1,128)} %bitcast.5, bf16[8192,256]{1,0:T(8,128)(2,1)} %pool_hbm.1, bf16[8192,256]{1,0:T(8,128)(2,1)} %cen_hbm.1, ...), custom_call_target="tpu_custom_call" | custom-call | tf_op jit(solution)/shard_map/pallas_call | solution.py:313
  94.8 1.9 %copy.15 = f32[16,8192]{1,0:T(8,128)} copy(f32[16,8192]{1,0:T(8,128)} %get-tuple-element.4) | data formatting | bytes 1048576
  96.7 1.6 %copy.16 = f32[16,2048]{1,0:T(8,128)} copy(f32[16,2048]{1,0:T(8,128)} %get-tuple-element.5) | data formatting | bytes 262144
  (2 shorter events, 0.0 us)

commit v2 on v1

--- a/solution.py
+++ b/solution.py
@@ -24,10 +24,10 @@
 
 def kernel(
     nl, nc, nch,
-    lidx_ref, nys_ref, targets_ref, eig_ref, damp_ref, pool_hbm, cen_hbm, w_hbm,
+    index_ref, nys_ref, targets_ref, eig_ref, damp_ref, pool_hbm, cen_hbm, w_hbm,
     out_ref, pred_ref,
     pool, cen, w, w_half, kern, cen_b, rows2, row_sq, batch, picked, pick_in, own,
-    part, rs_in, cg_in, quarter, resid, grad, co_in, co_in2, co_own,
+    part, rs_in, cg_in, quarter, resid, grad, co_in, co_in2, co_own, buf_a, buf_b,
     sem_in, s_pick, r_pick, s_bc, r_bc, s_x, r_x, s_rs, r_rs, s_cg, r_cg, s_lg, r_lg,
     s_c1, r_c1, s_c2, r_c2,
 ):
@@ -68,15 +68,22 @@
 
     loads[0].wait()
     held = pool.shape[0]
-    n_pick = lidx_ref.shape[0]
-    lidx = lidx_ref[...] - L * held
+    n_pick = nl * nch * PIECE
+    index = index_ref[...]
+    lanes = index.shape[1]
+    index = pltpu.roll(index, lax.rem(lanes - c * PIECE, lanes), 1)[:, :128] - L * held
+    if nch * nl < 8:
+        index = jnp.concatenate([index] * (8 // (nch * nl)), axis=0)
+    index = jnp.transpose(index)[:PIECE]
+    order = [k * nl + p for p in range(nl) for k in range(nch)]
+    lidx = jnp.concatenate([index[:, q:q + 1] for q in order], axis=0)
 
     def pick(t, acc):
         spot = lax.broadcasted_iota(jnp.int32, (n_pick, PT), 1) + t * PT
         hot = jnp.where(spot == lidx, 1.0, 0.0).astype(BF16)
         return acc + dot(hot, pool[pl.ds(pl.multiple_of(t * PT, PT), PT), :])
 
-    acc = lax.fori_loop(0, held // PT, pick, jnp.zeros((n_pick, pool.shape[1]), F32))
+    acc = lax.fori_loop(0, held // PT, pick, jnp.zeros((n_pick, pool.shape[1]), F32), unroll=2)
     picked[...] = acc.astype(BF16).reshape(picked.shape)
     pl.semaphore_wait(barrier, nl - 1 + nc - 1)
     copies = [
@@ -97,7 +104,7 @@
         cen_b[at, :] = dot(hi, ones) + dot(lo, ones)
         return carry
 
-    lax.fori_loop(0, n_cen // CT, norms, 0)
+    lax.fori_loop(0, n_cen // CT, norms, 0, unroll=2)
     loads[2].wait()
     w_half[...] = w[...].astype(BF16)
 
@@ -186,26 +193,45 @@
             lo = (sq - hi.astype(F32)).astype(BF16)
             row_sq[s] = dot(one, hi, NT) + dot(one, lo, NT)
 
-    def compute(k, half):
-        tiles = n_cen // CT // 2
+    def cross(s, t, buf):
+        at = pl.ds(pl.multiple_of(t * CT, CT), CT)
+        buf[...] = dot(cen[at, :], rows2[s], NT)
+
+    def values(k, s, t, buf):
+        at = pl.ds(pl.multiple_of(t * CT, CT), CT)
+        side = jnp.concatenate([cen_b[at, :]] * (SUB // 128), axis=1)
+        z = jnp.maximum(buf[...] + row_sq[s, 0:1, :] + side, 1e-30)
+        kern[k * n_sub + s, at, :] = jnp.exp2((z * lax.rsqrt(z)) * scale).astype(BF16)
+
+    def weigh(k, s, t):
+        at = pl.ds(pl.multiple_of(t * CT, CT), CT)
+        return dot(w_half[:, at], kern[k * n_sub + s, at, :])
+
+    tiles = n_cen // CT
+
+    def compute(k, between):
         for s in range(n_sub):
-            def step(t, acc):
-                at = pl.ds(pl.multiple_of((t + half * tiles) * CT, CT), CT)
-                cross = dot(cen[at, :], rows2[s], NT)
-                side = jnp.concatenate([cen_b[at, :]] * (SUB // 128), axis=1)
-                z = jnp.maximum(cross + row_sq[s, 0:1, :] + side, 1e-30)
-                val = jnp.exp2((z * lax.rsqrt(z)) * scale).astype(BF16)
-                kern[k * n_sub + s, at, :] = val
-                return acc + dot(w_half[:, at], val)
-
-            acc = lax.fori_loop(0, tiles, step, jnp.zeros((16, SUB), F32))
-            per = max(1, SUB // qw)
+            def step(u, acc):
+                t = 2 * u
+                before = weigh(k, s, jnp.maximum(t - 1, 0))
+                acc = acc + jnp.where(u > 0, before, 0.0)
+                cross(s, t + 1, buf_b)
+                values(k, s, t, buf_a)
+                cross(s, jnp.minimum(t + 2, tiles - 1), buf_a)
+                acc = acc + weigh(k, s, t)
+                values(k, s, t + 1, buf_b)
+                return acc
+
+            cross(s, 0, buf_a)
+            acc = lax.fori_loop(0, tiles // 4, step, jnp.zeros((16, SUB), F32))
+            if s == 0:
+                between()
+            acc = lax.fori_loop(tiles // 4, tiles // 2, step, acc)
+            acc = acc + weigh(k, s, tiles - 1)
             width = min(qw, SUB)
-            for q in range(per):
+            for q in range(SUB // width):
                 lo = s * SUB + q * width
-                dst = (k, lo // qw, slice(None), slice(lo % qw, lo % qw + width))
-                piece = acc[:, q * width:(q + 1) * width]
-                part[dst] = piece if half == 0 else part[dst] + piece
+                part[k, lo // qw, :, lo % qw:lo % qw + width] = acc[:, q * width:(q + 1) * width]
 
     def gradient(k):
         for s in range(n_sub):
@@ -220,7 +246,7 @@
                     grad[:, at] = grad[:, at] + term
                 return carry
 
-            lax.fori_loop(0, n_cen // GT, step, 0)
+            lax.fori_loop(0, n_cen // GT, step, 0, unroll=2)
 
     x_send(0)
     x_forward(0)
@@ -229,12 +255,14 @@
         x_send(1)
     for k in range(nch):
         prepare(k)
-        compute(k, 0)
-        if k + 1 < nch:
-            x_forward(k + 1)
-        if k >= 1:
-            ar_mid(k - 1)
-        compute(k, 1)
+
+        def between():
+            if k + 1 < nch:
+                x_forward(k + 1)
+            if k >= 1:
+                ar_mid(k - 1)
+
+        compute(k, between)
         if k + 1 < nch:
             x_done(k + 1)
         if k + 2 < nch:
@@ -304,9 +332,7 @@
     width = centers.shape[1]
     n_cen = centers.shape[0]
     qw = nc * PIECE
-    index = batch_index.reshape(nch, nl, nc, PIECE)
-    index = lax.dynamic_slice_in_dim(index, lax.axis_index("centers"), 1, axis=2)
-    lidx = jnp.transpose(index[:, :, 0, :], (1, 0, 2)).reshape(nl * nch * PIECE, 1)
+    index = batch_index.reshape(nch * nl, nc * PIECE)
     dma = lambda *s: [pltpu.SemaphoreType.DMA(s), pltpu.SemaphoreType.DMA(s)]
     vmem = pl.BlockSpec(memory_space=pltpu.VMEM)
     hbm = pl.BlockSpec(memory_space=pl.ANY)
@@ -340,6 +366,8 @@
             pltpu.VMEM((nl, 16, 128), F32),
             pltpu.VMEM((nc, 16, 128), F32),
             pltpu.VMEM((2, 16, 128), F32),
+            pltpu.VMEM((CT, SUB), F32),
+            pltpu.VMEM((CT, SUB), F32),
             pltpu.SemaphoreType.DMA((3,)),
             *dma(nl - 1), *dma(nch, nc - 1), *dma(nch, 3), *dma(nch, nl - 1),
             *dma(nch, nc - 1), *dma(nch, nl - 1), *dma(nl - 1), *dma(nc - 1),
@@ -347,7 +375,7 @@
         compiler_params=pltpu.CompilerParams(
             collective_id=0, has_side_effects=True, vmem_limit_bytes=62 * 1024 * 1024
         ),
-    )(lidx, nys_index, targets, eigvecs, damping.reshape(1, -1), pool, centers, weights)
+    )(index, nys_index, targets, eigvecs, damping.reshape(1, -1), pool, centers, weights)
     return (fresh, predictions)
 
 

time: 98.5 us -> 86.5 us (0.88)
  Pallas kernels: 92.6 us -> 82.2 us
  local copies, waits for them, and re-layouts: 4.99 us -> 3.44 us
    pallas_call x1, Pallas kernels: 92.6 us -> 82.2 us  [body(): pl.pallas_call(functools.partial(kernel, nl, nc, nch), out_shape=(jax.Sha...]
    reshape x2 -> x0, local copies, waits for them, and re-layouts: 1.53 us -> none  [the longest x1 0.77 us: body(): index = batch_index.reshape(nch, nl, nc, PIECE)]
where the time goes in v2:
time: 86.5 us; the launch traced here: 86.3 us
  Pallas kernels  82.2 us (95%)
  local copies, waits for them, and re-layouts  3.44 us (4%)
    pallas_call x1, Pallas kernels, body(): pl.pallas_call(functools.partial(kernel, nl, nc, nch), out_shape=(jax.Sha...  82.2 us
    unnamed x2, local copies, waits for them, and re-layouts  3.44 us

profile of v2, /device:TPU:0, one launch (start us, length us, event | category | flops | bytes accessed | tf_op | source)
XLA Modules:
  0.0 86.3 jit_solution(12242353476204198147)
XLA Ops:
  0.6 82.2 %shard_map.95 = (f32[16,8192]{1,0:T(8,128)}, f32[16,2048]{1,0:T(8,128)}) custom-call(s32[16,128]{1,0:T(8,128)} %bitcast.2, s32[64]{0:T(128)} %nys_ref.1, f32[16,2048]{1,0:T(8,128)} %targets_ref.1, f32[64,128]{1,0:T(8,128)} %eig_ref.1, f32[1,128]{1,0:T(1,128)} %bitcast.3, bf16[8192,256]{1,0:T(8,128)(2,1)} %pool_hbm.1, bf16[8192,256]{1,0:T(8,128)(2,1)} %cen_hbm.1, ...), custom_call_target="tpu_custom_call" | custom-call | tf_op jit(solution)/shard_map/pallas_call | solution.py:339
  82.9 1.9 %copy.12 = f32[16,8192]{1,0:T(8,128)} copy(f32[16,8192]{1,0:T(8,128)} %get-tuple-element.4) | data formatting | bytes 1048576
  84.7 1.6 %copy.13 = f32[16,2048]{1,0:T(8,128)} copy(f32[16,2048]{1,0:T(8,128)} %get-tuple-element.5) | data formatting | bytes 262144

commit v3 on v2

--- a/solution.py
+++ b/solution.py
@@ -25,9 +25,9 @@
 def kernel(
     nl, nc, nch,
     index_ref, nys_ref, targets_ref, eig_ref, damp_ref, pool_hbm, cen_hbm, w_hbm,
-    out_ref, pred_ref,
+    grad, pred_ref, coeff_ref,
     pool, cen, w, w_half, kern, cen_b, rows2, row_sq, batch, picked, pick_in, own,
-    part, rs_in, cg_in, quarter, resid, grad, co_in, co_in2, co_own, buf_a, buf_b,
+    part, rs_in, cg_in, quarter, resid, nys_rows, nys_kern, co_in, co_in2, co_own, buf_a, buf_b,
     sem_in, s_pick, r_pick, s_bc, r_bc, s_x, r_x, s_rs, r_rs, s_cg, r_cg, s_lg, r_lg,
     s_c1, r_c1, s_c2, r_c2,
 ):
@@ -105,6 +105,19 @@
         return carry
 
     lax.fori_loop(0, n_cen // CT, norms, 0, unroll=2)
+
+    n_nys = eig_ref.shape[0]
+    in_block = lax.broadcasted_iota(jnp.int32, (128, cen.shape[1]), 0)
+
+    def nystrom(j, carry):
+        rows = cen[pl.ds(pl.multiple_of(j * 128, 128), 128), :].astype(F32)
+        rows = jnp.where(in_block == nys_ref[j] - j * 128, rows, 0.0)
+        nys_rows[pl.ds(j, 1), :] = jnp.sum(rows, axis=0, keepdims=True)
+        return carry
+
+    lax.fori_loop(0, n_nys, nystrom, 0, unroll=4)
+    nys_cen = nys_rows[...].astype(BF16)
+    nys_sq = jnp.sum(nys_rows[...] * nys_rows[...], axis=1, keepdims=True)
     loads[2].wait()
     w_half[...] = w[...].astype(BF16)
 
@@ -178,30 +191,32 @@
             lo = k * chunk + p * qw
             pred_ref[:, lo:lo + qw] = quarter[k, p]
             diff = quarter[k, p] - targets_ref[:, lo:lo + qw]
-            resid[:, lo:lo + qw] = diff.astype(BF16)
-
-    scale = -4.0 / math.sqrt(cen.shape[1]) * math.log2(math.e)
+            resid[:, lo:lo + qw] = -2.0 * diff.astype(BF16)
+
+    scale = -4.0 / math.sqrt(cen.shape[1])
 
     def prepare(k):
         one = jnp.ones((8, cen.shape[1]), BF16)
         rows = batch[k].reshape(chunk, cen.shape[1])
         for s in range(n_sub):
             r = rows[s * SUB:(s + 1) * SUB].astype(F32)
-            rows2[s] = (-2.0 * r).astype(BF16)
+            rows2[s] = jnp.transpose((-2.0 * r).astype(BF16))
             sq = r * r
             hi = sq.astype(BF16)
             lo = (sq - hi.astype(F32)).astype(BF16)
             row_sq[s] = dot(one, hi, NT) + dot(one, lo, NT)
+            z = jnp.maximum(dot(nys_cen, rows2[s]) + row_sq[s, 0:1, :] + nys_sq, 1e-30)
+            nys_kern[k * n_sub + s] = jnp.exp((z * lax.rsqrt(z)) * scale).astype(BF16)
 
     def cross(s, t, buf):
         at = pl.ds(pl.multiple_of(t * CT, CT), CT)
-        buf[...] = dot(cen[at, :], rows2[s], NT)
+        buf[...] = dot(cen[at, :], rows2[s])
 
     def values(k, s, t, buf):
         at = pl.ds(pl.multiple_of(t * CT, CT), CT)
         side = jnp.concatenate([cen_b[at, :]] * (SUB // 128), axis=1)
         z = jnp.maximum(buf[...] + row_sq[s, 0:1, :] + side, 1e-30)
-        kern[k * n_sub + s, at, :] = jnp.exp2((z * lax.rsqrt(z)) * scale).astype(BF16)
+        kern[k * n_sub + s, at, :] = jnp.exp((z * lax.rsqrt(z)) * scale).astype(BF16)
 
     def weigh(k, s, t):
         at = pl.ds(pl.multiple_of(t * CT, CT), CT)
@@ -233,7 +248,9 @@
                 lo = s * SUB + q * width
                 part[k, lo // qw, :, lo % qw:lo % qw + width] = acc[:, q * width:(q + 1) * width]
 
-    def gradient(k):
+    gt = n_cen // GT
+
+    def gradient(k, first=0, end=gt):
         for s in range(n_sub):
             lo = k * chunk + s * SUB
 
@@ -241,12 +258,12 @@
                 at = pl.ds(pl.multiple_of(t * GT, GT), GT)
                 term = dot(resid[:, lo:lo + SUB], kern[k * n_sub + s, at, :], NT)
                 if lo == 0:
-                    grad[:, at] = term
+                    grad[:, at] = w[:, at] + term
                 else:
                     grad[:, at] = grad[:, at] + term
                 return carry
 
-            lax.fori_loop(0, n_cen // GT, step, 0, unroll=2)
+            lax.fori_loop(first, end, step, 0, unroll=2)
 
     x_send(0)
     x_forward(0)
@@ -283,23 +300,18 @@
         residual(k)
         gradient(k)
     residual(last)
-    gradient(last)
-
-    n_nys = eig_ref.shape[0]
-    lane = lax.broadcasted_iota(jnp.int32, (16, 128), 1)
-
-    def coeff_step(j, acc):
-        at = pl.ds(pl.multiple_of(j * 128, 128), 128)
-        hit = lane == nys_ref[j] - j * 128
-        g = jnp.sum(jnp.where(hit, grad[:, at], 0.0), axis=1, keepdims=True)
-        return acc + g * eig_ref[pl.ds(j, 1), :]
-
-    co_own[0] = lax.fori_loop(0, n_nys, coeff_step, jnp.zeros((16, 128), F32), unroll=8)
+    nys_grad = jnp.zeros((16, n_nys), F32)
+    for q in range(nch * n_sub):
+        nys_grad = nys_grad + dot(resid[:, q * SUB:(q + 1) * SUB], nys_kern[q], NT)
+    co_own[0] = lax.dot_general(
+        nys_grad, eig_ref[...], NN, precision=lax.Precision.HIGHEST, preferred_element_type=F32
+    )
     c1 = [
         send(co_own.at[0], co_in.at[L], s_c1.at[d], r_c1.at[d], p, c)
         for d, p in enumerate(lpeer)
     ]
     co_in[L] = co_own[0]
+    gradient(last, 0, gt // 2)
     for copy in c1:
         copy.wait_recv()
     co_own[1] = sum((co_in[p] for p in range(1, nl)), co_in[0])
@@ -308,20 +320,25 @@
         for d, p in enumerate(cpeer)
     ]
     co_in2[c] = co_own[1]
+    gradient(last, gt // 2, gt)
     for copy in c2:
         copy.wait_recv()
-    coeff = sum((co_in2[p] for p in range(1, nc)), co_in2[0]) * damp_ref[...]
-
-    def final_step(j, carry):
-        at = pl.ds(pl.multiple_of(j * 128, 128), 128)
-        hit = lane == nys_ref[j] - j * 128
-        d = jnp.sum(coeff * eig_ref[pl.ds(j, 1), :], axis=1, keepdims=True)
-        out_ref[:, at] = w[:, at] - 2.0 * grad[:, at] + jnp.where(hit, 2.0 * d, 0.0)
-        return carry
-
-    lax.fori_loop(0, n_nys, final_step, 0, unroll=8)
+    coeff_ref[...] = sum((co_in2[p] for p in range(1, nc)), co_in2[0]) * damp_ref[...]
+
     for copy in started:
         copy.wait_send()
+
+
+def finish(nys_ref, eig_ref, coeff_ref, grad_ref, pred_ref, out_ref, pred_out):
+    pred_out[...] = pred_ref[...]
+    lane = lax.broadcasted_iota(jnp.int32, (16, 128), 1)
+    delta = lax.dot_general(
+        coeff_ref[...], eig_ref[...], NT, precision=lax.Precision.HIGHEST, preferred_element_type=F32
+    )
+    for j in range(eig_ref.shape[0]):
+        lo = j * 128
+        hit = lane == nys_ref[j] - lo
+        out_ref[:, lo:lo + 128] = grad_ref[:, lo:lo + 128] - jnp.where(hit, delta[:, j:j + 1], 0.0)
 
 
 def body(pool, batch_index, targets, centers, weights, nys_index, eigvecs, damping):
@@ -331,19 +348,22 @@
     chunk = rows // nch
     width = centers.shape[1]
     n_cen = centers.shape[0]
+    n_nys = nys_index.shape[0]
     qw = nc * PIECE
     index = batch_index.reshape(nch * nl, nc * PIECE)
     dma = lambda *s: [pltpu.SemaphoreType.DMA(s), pltpu.SemaphoreType.DMA(s)]
     vmem = pl.BlockSpec(memory_space=pltpu.VMEM)
     hbm = pl.BlockSpec(memory_space=pl.ANY)
-    fresh, predictions = pl.pallas_call(
+    smem = pl.BlockSpec(memory_space=pltpu.SMEM)
+    grad, pred, coeff = pl.pallas_call(
         functools.partial(kernel, nl, nc, nch),
         out_shape=(
             jax.ShapeDtypeStruct(weights.shape, F32),
             jax.ShapeDtypeStruct(targets.shape, F32),
+            jax.ShapeDtypeStruct((16, eigvecs.shape[1]), F32),
         ),
-        in_specs=[vmem, pl.BlockSpec(memory_space=pltpu.SMEM), vmem, vmem, vmem, hbm, hbm, hbm],
-        out_specs=(vmem, vmem),
+        in_specs=[vmem, smem, vmem, vmem, vmem, hbm, hbm, hbm],
+        out_specs=(vmem, vmem, vmem),
         scratch_shapes=[
             pltpu.VMEM(pool.shape, BF16),
             pltpu.VMEM(centers.shape, BF16),
@@ -351,7 +371,7 @@
             pltpu.VMEM(weights.shape, BF16),
             pltpu.VMEM((rows // SUB, n_cen, SUB), BF16),
             pltpu.VMEM((n_cen, 128), F32),
-            pltpu.VMEM((chunk // SUB, SUB, width), BF16),
+            pltpu.VMEM((chunk // SUB, width, SUB), BF16),
             pltpu.VMEM((chunk // SUB, 8, SUB), F32),
             pltpu.VMEM((nch, nl, qw, width), BF16),
             pltpu.VMEM((nl, nch * PIECE, width), BF16),
@@ -362,7 +382,8 @@
             pltpu.VMEM((nch, nc, 16, qw), F32),
             pltpu.VMEM((nch, nl, 16, qw), F32),
             pltpu.VMEM((16, rows), BF16),
-            pltpu.VMEM(weights.shape, F32),
+            pltpu.VMEM((n_nys, width), F32),
+            pltpu.VMEM((rows // SUB, n_nys, SUB), BF16),
             pltpu.VMEM((nl, 16, 128), F32),
             pltpu.VMEM((nc, 16, 128), F32),
             pltpu.VMEM((2, 16, 128), F32),
@@ -376,7 +397,15 @@
             collective_id=0, has_side_effects=True, vmem_limit_bytes=62 * 1024 * 1024
         ),
     )(index, nys_index, targets, eigvecs, damping.reshape(1, -1), pool, centers, weights)
-    return (fresh, predictions)
+    return pl.pallas_call(
+        finish,
+        out_shape=(
+            jax.ShapeDtypeStruct(weights.shape, F32),
+            jax.ShapeDtypeStruct(targets.shape, F32),
+        ),
+        in_specs=[smem, vmem, vmem, vmem, vmem],
+        out_specs=(vmem, vmem),
+    )(nys_index, eigvecs, coeff, grad, pred)
 
 
 def solution(mesh):

time: 86.5 us -> 84.5 us (0.977)
  local copies, waits for them, and re-layouts: 3.44 us -> 0 us
  Pallas kernels: 82.2 us -> 83.7 us
    unnamed x2 -> x0, local copies, waits for them, and re-layouts: 3.44 us -> none
    pallas_call x0 -> x1, Pallas kernels: none -> 2.36 us  [body(): pl.pallas_call(finish, out_shape=(jax.ShapeDtypeStruct(weights.shape, F32...]
    pallas_call x1, Pallas kernels: 82.2 us -> 81.3 us  [body(): pl.pallas_call(functools.partial(kernel, nl, nc, nch), out_shape=(jax.Sha...]
where the time goes in v3:
time: 84.5 us; the launch traced here: 84.3 us
  Pallas kernels  83.7 us (99%)
    pallas_call x1, Pallas kernels, body(): pl.pallas_call(functools.partial(kernel, nl, nc, nch), out_shape=(jax.Sha...  81.3 us
    pallas_call x1, Pallas kernels, body(): pl.pallas_call(finish, out_shape=(jax.ShapeDtypeStruct(weights.shape, F32...  2.36 us

profile of v3, /device:TPU:0, one launch (start us, length us, event | category | flops | bytes accessed | tf_op | source)
XLA Modules:
  0.0 84.3 jit_solution(834549467888983164)
XLA Ops:
  0.6 81.3 %shard_map.95 = (f32[16,8192]{1,0:T(8,128)}, f32[16,2048]{1,0:T(8,128)}, f32[16,128]{1,0:T(8,128)}) custom-call(s32[16,128]{1,0:T(8,128)} %bitcast.2, s32[64]{0:T(128)} %nys_ref.3, f32[16,2048]{1,0:T(8,128)} %targets_ref.1, f32[64,128]{1,0:T(8,128)} %eig_ref.3, f32[1,128]{1,0:T(1,128)} %bitcast.3, bf16[8192,256]{1,0:T(8,128)(2,1)} %pool_hbm.1, ...), custom_call_target="tpu_custom_call" | custom-call | tf_op jit(solution)/shard_map/pallas_call | solution.py:358
  82.0 2.4 %shard_map.96 = (f32[16,8192]{1,0:T(8,128)}, f32[16,2048]{1,0:T(8,128)}) custom-call(s32[64]{0:T(128)} %nys_ref.3, f32[64,128]{1,0:T(8,128)} %eig_ref.3, f32[16,128]{1,0:T(8,128)} %get-tuple-element.5.coeff_ref, f32[16,8192]{1,0:T(8,128)} %get-tuple-element.6.grad_ref, f32[16,2048]{1,0:T(8,128)} %get-tuple-element.7.pred_ref), custom_call_target="tpu_custom_call" | custom-call | tf_op jit(solution)/shard_map/pallas_call | solution.py:400

commit v4 on v3

--- a/solution.py
+++ b/solution.py
@@ -12,6 +12,7 @@
 SUB = 512
 CT = 512
 GT = 1024
+STRIP = 16
 PT = 512
 F32, BF16 = jnp.float32, jnp.bfloat16
 NT = (((1,), (1,)), ((), ()))
@@ -96,7 +97,7 @@
     ones = jnp.ones((cen.shape[1], 128), BF16)
 
     def norms(t, carry):
-        at = pl.ds(pl.multiple_of(t * CT, CT), CT)
+        at = pl.ds(pl.multiple_of(t * 128, 128), 128)
         sq = cen[at, :].astype(F32)
         sq = sq * sq
         hi = sq.astype(BF16)
@@ -104,7 +105,7 @@
         cen_b[at, :] = dot(hi, ones) + dot(lo, ones)
         return carry
 
-    lax.fori_loop(0, n_cen // CT, norms, 0, unroll=2)
+    lax.fori_loop(0, n_cen // 128, norms, 0, unroll=4)
 
     n_nys = eig_ref.shape[0]
     in_block = lax.broadcasted_iota(jnp.int32, (128, cen.shape[1]), 0)
@@ -213,10 +214,12 @@
         buf[...] = dot(cen[at, :], rows2[s])
 
     def values(k, s, t, buf):
-        at = pl.ds(pl.multiple_of(t * CT, CT), CT)
-        side = jnp.concatenate([cen_b[at, :]] * (SUB // 128), axis=1)
-        z = jnp.maximum(buf[...] + row_sq[s, 0:1, :] + side, 1e-30)
-        kern[k * n_sub + s, at, :] = jnp.exp((z * lax.rsqrt(z)) * scale).astype(BF16)
+        row = jnp.broadcast_to(row_sq[s, 0:1, :], (STRIP, SUB))
+        for i in range(CT // STRIP):
+            at = pl.ds(pl.multiple_of(t * CT + i * STRIP, STRIP), STRIP)
+            side = jnp.concatenate([cen_b[at, :]] * (SUB // 128), axis=1)
+            z = jnp.maximum(buf[i * STRIP:(i + 1) * STRIP, :] + row + side, 1e-30)
+            kern[k * n_sub + s, at, :] = jnp.exp((z * lax.rsqrt(z)) * scale).astype(BF16)
 
     def weigh(k, s, t):
         at = pl.ds(pl.multiple_of(t * CT, CT), CT)

time: 84.5 us -> 84.3 us (level)
  no operation moved by 1% of the time
where the time goes in v4:
time: 84.3 us; the launch traced here: 84.2 us
  Pallas kernels  83.5 us (99%)
    pallas_call x1, Pallas kernels, body(): pl.pallas_call(functools.partial(kernel, nl, nc, nch), out_shape=(jax.Sha...  81.2 us
    pallas_call x1, Pallas kernels, body(): pl.pallas_call(finish, out_shape=(jax.ShapeDtypeStruct(weights.shape, F32...  2.36 us

profile of v4, /device:TPU:0, one launch (start us, length us, event | category | flops | bytes accessed | tf_op | source)
XLA Modules:
  0.0 84.2 jit_solution(17651654062785744625)
XLA Ops:
  0.6 81.2 %shard_map.95 = (f32[16,8192]{1,0:T(8,128)}, f32[16,2048]{1,0:T(8,128)}, f32[16,128]{1,0:T(8,128)}) custom-call(s32[16,128]{1,0:T(8,128)} %bitcast.2, s32[64]{0:T(128)} %nys_ref.3, f32[16,2048]{1,0:T(8,128)} %targets_ref.1, f32[64,128]{1,0:T(8,128)} %eig_ref.3, f32[1,128]{1,0:T(1,128)} %bitcast.3, bf16[8192,256]{1,0:T(8,128)(2,1)} %pool_hbm.1, ...), custom_call_target="tpu_custom_call" | custom-call | tf_op jit(solution)/shard_map/pallas_call | solution.py:361
  81.8 2.4 %shard_map.96 = (f32[16,8192]{1,0:T(8,128)}, f32[16,2048]{1,0:T(8,128)}) custom-call(s32[64]{0:T(128)} %nys_ref.3, f32[64,128]{1,0:T(8,128)} %eig_ref.3, f32[16,128]{1,0:T(8,128)} %get-tuple-element.5.coeff_ref, f32[16,8192]{1,0:T(8,128)} %get-tuple-element.6.grad_ref, f32[16,2048]{1,0:T(8,128)} %get-tuple-element.7.pred_ref), custom_call_target="tpu_custom_call" | custom-call | tf_op jit(solution)/shard_map/pallas_call | solution.py:403
